TPU v7x, 32 devices: a whole 2x2x4 slice. The times are simulated.
32 devices in a mesh: groups: 2 (over y), expert: 4 (over z), head: 4 (over x, core).
Axes of the slice: x: 2, y: 2, z: 4, core: 2. Of those that a mesh axis runs over, the one named last changes fastest.
Arguments:
- tokens: bfloat16 [2, 32, 7168], P(None, ('groups', 'expert'), 'head'), parts along dimension 1, may hold values from -6 to 6
- gate_scores: float32 [2, 32, 2], P(None, ('groups', 'expert')), parts along dimension 1, may hold values from 0.05 to 1
- route_copy: int32 [2, 32, 2], P(None, ('groups', 'expert')), parts along dimension 1, may hold values from 0 to 3, as said below
- gate_up: bfloat16 [4, 7168, 2, 1024], P('expert', 'head'), as said below
- down_proj: bfloat16 [4, 1024, 7168], P('expert', None, 'head')
Outputs:
- combined: bfloat16 [2, 32, 7168], P(None, ('groups', 'expert'), 'head'), parts along dimension 1
There are 2 independent parts, one for each index of `groups`. A program takes and returns all parts, laid end to end along the dimension named above; an argument that names none is the same for every part. Nothing has to cross between parts.
Inputs may be any that keep to these rules, and one draw needn't show every extreme that they name: Each of the 3 experts is held by one or two slots; slots that hold the same expert hold equal projections in gate_up and down_proj. `route_copy`: the 2 copies named by one row are different. In one step, at most 4 entries of the rows of one index of expert name the same copy; in every draw some copies receive exactly 4 entries from the rows of every index of expert.
All inputs are finite; a program needn't handle non-finite values.
Results may differ from a plain program's by a relative error of at most 0.0049.
Values may be sent and summed in bfloat16 or wider, within the bound.
A program may use at most 64 MiB of HBM per device.

v0:
```python
import jax
import jax.numpy as jnp
from jax import lax
from jax.sharding import PartitionSpec as P


def body(tokens, gate_scores, route_copy, gate_up, down_proj):
    device_count = lax.axis_size("expert")
    row_count = tokens.shape[1]
    quarter = tokens.shape[2]
    top_count = route_copy.shape[2]
    span_count = max(1, device_count // 16)
    slot_count = device_count // span_count
    per_copy = 2 * row_count * top_count // slot_count
    unit_count = gate_up.shape[3]
    w_in = gate_up.reshape(quarter, 2 * unit_count)
    w_out = down_proj.reshape(unit_count, quarter)
    outputs = []
    for index in range(tokens.shape[0]):
        step_tokens = tokens[index : index + 1]
        scores = gate_scores[index : index + 1]
        step_span = step_tokens.shape[0]
        entries = row_count * top_count
        route_item_count = step_span * per_copy
        flat_copies = route_copy[index : index + 1].reshape(step_span, entries)
        onehot = (flat_copies[:, :, None] == jnp.arange(slot_count, dtype=jnp.int32)).astype(
            jnp.int32
        )
        position = jnp.sum(onehot * jnp.cumsum(onehot, axis=1), axis=2) - 1
        step_ids = jnp.arange(step_span, dtype=jnp.int32)[:, None]
        target = flat_copies * route_item_count + step_ids * per_copy + position
        target = target.reshape(step_span * row_count, top_count)
        places = jnp.arange(slot_count * route_item_count, dtype=jnp.int32)
        selector = jnp.any(places[:, None, None] == target[None], axis=2).astype(jnp.bfloat16)
        weights = 2.5 * scores / jnp.sum(scores, axis=2, keepdims=True)
        weights = weights.reshape(step_span * row_count, top_count)
        mixing = jnp.sum(jnp.where(target[:, :, None] == places, weights[:, :, None], 0.0), axis=1)
        packed = jnp.dot(
            selector,
            step_tokens.reshape(step_span * row_count, quarter),
            preferred_element_type=jnp.float32,
        )
        packed = packed.astype(jnp.bfloat16).reshape(slot_count, 1, route_item_count, quarter)
        outgoing = jnp.broadcast_to(packed, (slot_count, span_count, route_item_count, quarter))
        outgoing = outgoing.reshape(device_count, route_item_count, quarter)
        rows_in = lax.all_to_all(outgoing, "expert", split_axis=0, concat_axis=0, tiled=True)
        item_count = rows_in.shape[1]
        expert_gated = jnp.dot(
            rows_in.reshape(-1, quarter), w_in, preferred_element_type=jnp.float32
        )
        total = lax.psum(expert_gated, "head")
        hidden = (jax.nn.silu(total[:, :unit_count]) * total[:, unit_count:]).astype(jnp.bfloat16)
        partial_value = jnp.dot(hidden, w_out, preferred_element_type=jnp.float32)
        partial_value = partial_value.reshape(device_count, item_count, quarter)
        back = lax.all_to_all(partial_value, "expert", split_axis=0, concat_axis=0, tiled=True)
        returned = jnp.sum(back.reshape(slot_count, span_count, item_count, quarter), axis=1)
        summed = jnp.dot(mixing, returned.reshape(-1, quarter), precision=lax.Precision.HIGHEST)
        outputs.append(summed.reshape(step_span, row_count, quarter).astype(jnp.bfloat16))
    combined = jnp.concatenate(outputs, axis=0)
    return combined


def solution(mesh):
    return jax.shard_map(
        body,
        mesh=mesh,
        in_specs=(
            P(None, ("groups", "expert"), "head"),
            P(None, ("groups", "expert"), None),
            P(None, ("groups", "expert"), None),
            P("expert", "head", None, None),
            P("expert", None, "head"),
        ),
        out_specs=P(None, ("groups", "expert"), "head"),
        check_vma=False,
    )
```

profile of v0, /device:TPU:0, one launch (start us, length us, event | category | flops | bytes accessed | tf_op | source)
XLA Modules:
  0.0 109.3 jit_solution(2964968552188497278)
XLA Ops:
  6.5 0.7 fusion.18
  7.2 0.1 copy.43
  7.4 0.2 reduce_window_sum.18
  7.7 0.1 copy.41
  7.9 0.9 convolution_convert_fusion
  8.8 0.6 reshape_reshape.7
  9.5 6.3 %all-to-all-start.2 = ((bf16[4,4,1792]{2,1,0:T(4,128)(2,1)}), bf16[4,4,1792]{2,1,0:T(4,128)(2,1)S(1)}, u32[]{:S(2)}, u32[]{:S(2)}) async-start(bf16[4,4,1792]{2,1,0:T(4,128)(2,1)} %reshape_reshape.7), calls=%async_computation.2 | async-start | bytes 114688 | tf_op jit(solution)/shard_map/all_to_all | solution.py:46
  15.9 0.7 slice_reduce_fusion.1
  16.6 0.1 copy.42
  16.8 0.1 copy.39
  16.8 0.1 copy.40
  16.9 0.2 reduce_window_sum.17
  17.2 0.1 copy.37
  17.4 0.9 convolution_convert_fusion.1
  18.3 0.7 divide_bitcast_fusion.1
  19.3 0.6 reshape_reshape.6
  20.0 9.1 %copy.44 = bf16[224,8,2,1024]{3,1,2,0:T(8,128)(2,1)} copy(bf16[224,8,2,1024]{3,2,1,0:T(2,128)(2,1)} %bitcast.43) | data formatting | bytes 14680064
  29.1 5.1 %all-to-all-start = ((bf16[4,4,1792]{2,1,0:T(4,128)(2,1)}), bf16[4,4,1792]{2,1,0:T(4,128)(2,1)S(1)}, u32[]{:S(2)}, u32[]{:S(2)}) async-start(bf16[4,4,1792]{2,1,0:T(4,128)(2,1)} %reshape_reshape.6), calls=%async_computation | async-start | bytes 114688 | tf_op jit(solution)/shard_map/all_to_all | solution.py:46
  34.2 4.8 %fusion.20 = f32[16,2048]{1,0:T(8,128)} fusion(bf16[16,1792]{1,0:T(8,128)(2,1)S(1)} %reshape.306, bf16[1792,2048]{1,0:T(8,128)(2,1)} %bitcast.41), kind=kOutput, calls=%fused_computation.47 | convolution fusion | flops 117440512 | bytes 7528448 | tf_op jit(solution)/shard_map/dot_general | solution.py:48
  39.0 0.9 all-to-all-done
  39.9 4.8 %fusion.19 = f32[16,2048]{1,0:T(8,128)} fusion(bf16[16,1792]{1,0:T(8,128)(2,1)S(1)} %reshape.301, bf16[1792,2048]{1,0:T(8,128)(2,1)} %bitcast.42), kind=kOutput, calls=%fused_computation.46 | convolution fusion | flops 117440512 | bytes 7528448 | tf_op jit(solution)/shard_map/dot_general | solution.py:48
  44.8 32.8 %all-reduce.3.cloned.1.call-done = (f32[16,2048]{1,0:T(8,128)}, f32[16,2048]{1,0:T(8,128)}) async-done(((f32[16,2048]{1,0:T(8,128)}, f32[16,2048]{1,0:T(8,128)}), (f32[16,2048]{1,0:T(8,128)}, f32[16,2048]{1,0:T(8,128)})) %all-reduce.3.cloned.1.call-update) | async-done | bytes 262160 | tf_op jit(solution)/shard_map/psum | solution.py:51
  77.6 1.0 fusion.6
  78.6 3.3 %fusion.2 = f32[4,4,1792]{2,1,0:T(4,128)} fusion(bf16[4,4,1024]{2,1,0:T(4,128)(2,1)S(1)} %dot_general.30, bf16[1,1024,1792]{2,1,0:T(8,128)(2,1)} %param.9), kind=kOutput, calls=%fused_computation.2 | convolution fusion | flops 58720256 | bytes 3817472 | tf_op jit(solution)/shard_map/dot_general | solution.py:53
  81.9 4.6 %all-to-all-start.1 = ((f32[4,4,1792]{2,1,0:T(4,128)}), f32[4,4,1792]{2,1,0:T(4,128)S(1)}, u32[]{:S(2)}, u32[]{:S(2)}) async-start(f32[4,4,1792]{2,1,0:T(4,128)} %fusion.2), calls=%async_computation.1 | async-start | bytes 229376 | tf_op jit(solution)/shard_map/all_to_all | solution.py:55
  86.5 3.3 %fusion = f32[4,4,1792]{2,1,0:T(4,128)} fusion(bf16[4,4,1024]{2,1,0:T(4,128)(2,1)S(1)} %dot_general.35, bf16[1,1024,1792]{2,1,0:T(8,128)(2,1)} %param.9), kind=kOutput, calls=%fused_computation | convolution fusion | flops 58720256 | bytes 3817472 | tf_op jit(solution)/shard_map/dot_general | solution.py:53
  89.8 2.6 %all-to-all-done.1 = f32[4,4,1792]{2,1,0:T(4,128)S(1)} async-done(((f32[4,4,1792]{2,1,0:T(4,128)}), f32[4,4,1792]{2,1,0:T(4,128)S(1)}, u32[]{:S(2)}, u32[]{:S(2)}) %all-to-all-start.1) | async-done | bytes 114720 | tf_op jit(solution)/shard_map/all_to_all | solution.py:55
  92.4 3.3 %all-to-all-start.3 = ((f32[4,4,1792]{2,1,0:T(4,128)}), f32[4,4,1792]{2,1,0:T(4,128)S(1)}, u32[]{:S(2)}, u32[]{:S(2)}) async-start(f32[4,4,1792]{2,1,0:T(4,128)} %fusion), calls=%async_computation.3 | async-start | bytes 229376 | tf_op jit(solution)/shard_map/all_to_all | solution.py:55
  95.8 0.2 fusion.4
  96.0 5.5 %all-to-all-done.3 = f32[4,4,1792]{2,1,0:T(4,128)S(1)} async-done(((f32[4,4,1792]{2,1,0:T(4,128)}), f32[4,4,1792]{2,1,0:T(4,128)S(1)}, u32[]{:S(2)}, u32[]{:S(2)}) %all-to-all-start.3) | async-done | bytes 114720 | tf_op jit(solution)/shard_map/all_to_all | solution.py:55
  101.6 0.2 fusion.5
  101.8 0.6 pad_maximum_fusion
  (30 shorter events, 1.2 us)
Async XLA Ops:
  9.5 19.6 %all-to-all-start.2 = ((bf16[4,4,1792]{2,1,0:T(4,128)(2,1)}), bf16[4,4,1792]{2,1,0:T(4,128)(2,1)S(1)}, u32[]{:S(2)}, u32[]{:S(2)}) async-start(bf16[4,4,1792]{2,1,0:T(4,128)(2,1)} %reshape_reshape.7), calls=%async_computation.2 | async-start | bytes 114688 | tf_op jit(solution)/shard_map/all_to_all | solution.py:46
  29.1 10.8 %all-to-all-start = ((bf16[4,4,1792]{2,1,0:T(4,128)(2,1)}), bf16[4,4,1792]{2,1,0:T(4,128)(2,1)S(1)}, u32[]{:S(2)}, u32[]{:S(2)}) async-start(bf16[4,4,1792]{2,1,0:T(4,128)(2,1)} %reshape_reshape.6), calls=%async_computation | async-start | bytes 114688 | tf_op jit(solution)/shard_map/all_to_all | solution.py:46
  34.2 43.4 %all-reduce.3.cloned.1.call-start = ((), (), s32[]{:S(2)}) async-start(), calls=%async_computation.4 | async-start | bytes 524288 | tf_op jit(solution)/shard_map/psum | solution.py:51
  81.9 10.5 %all-to-all-start.1 = ((f32[4,4,1792]{2,1,0:T(4,128)}), f32[4,4,1792]{2,1,0:T(4,128)S(1)}, u32[]{:S(2)}, u32[]{:S(2)}) async-start(f32[4,4,1792]{2,1,0:T(4,128)} %fusion.2), calls=%async_computation.1 | async-start | bytes 229376 | tf_op jit(solution)/shard_map/all_to_all | solution.py:55
  92.4 9.2 %all-to-all-start.3 = ((f32[4,4,1792]{2,1,0:T(4,128)}), f32[4,4,1792]{2,1,0:T(4,128)S(1)}, u32[]{:S(2)}, u32[]{:S(2)}) async-start(f32[4,4,1792]{2,1,0:T(4,128)} %fusion), calls=%async_computation.3 | async-start | bytes 229376 | tf_op jit(solution)/shard_map/all_to_all | solution.py:55
Sparse Core Ops, SparseCore 0:
  44.9 32.6 all-reduce.2
where the time goes:
time: 110 us; the launch traced here: 109 us
  waiting for transfers between devices  41.8 us (38%)
  starting transfers between devices  19.3 us (18%)
  matrix products  18.4 us (17%)
  between operations  13.5 us (12%)
  local copies, waits for them, and re-layouts  12.5 us (11%)
  other arithmetic  3.74 us (3%)
    psum x1, waiting for transfers between devices, body(): total = lax.psum(expert_gated, 'head')  32.8 us
    all_to_all x2, starting transfers between devices, body(): lax.all_to_all(outgoing, 'expert', split_axis=0, concat_axis=0, tiled=True)  11.4 us
    dot_general x2, matrix products, body(): jnp.dot(rows_in.reshape(-1, quarter), w_in, preferred_element_type=jnp.fl...  9.59 us
    unnamed x3, local copies, waits for them, and re-layouts  9.31 us
    all_to_all x2, waiting for transfers between devices, body(): lax.all_to_all(partial_value, 'expert', split_axis=0, concat_axis=0, tile...  8.1 us
    all_to_all x2, starting transfers between devices, body(): lax.all_to_all(partial_value, 'expert', split_axis=0, concat_axis=0, tile...  7.91 us
    dot_general x2, matrix products, body(): partial_value = jnp.dot(hidden, w_out, preferred_element_type=jnp.float32)  6.6 us
  transfers between devices with their start and end apart: 5, of which 4 were waited for; matrix products, arithmetic and copies ran while one was open for 20% of the time, Pallas kernels for 0%

commit v1 on v0

v1 whole, which is shorter than its diff:
```python
import functools

import jax
import jax.numpy as jnp
from jax import lax
from jax.experimental import pallas as pl
from jax.experimental.pallas import tpu as pltpu
from jax.sharding import PartitionSpec as P

MESH = pl.DeviceIdType.MESH
F32, BF16 = jnp.float32, jnp.bfloat16


def widths_of(half):
    first = ((half // 128 + 1) // 2) * 128
    return [w for w in (first, half - first) if w]


def fused(
    experts,
    heads,
    span,
    tokens_ref,
    scores_ref,
    routes_ref,
    gate_up_ref,
    down_ref,
    out_ref,
    w_in,
    w_pairs,
    w_out,
    flat,
    packed,
    spread,
    share,
    sums,
    sums_out,
    sums_in,
    hidden_all,
    own,
    *rest,
):
    parts = (len(rest) - 10) // 2
    results_out, results_in = rest[:parts], rest[parts : 2 * parts]
    (w_sem, down_sem, tok_send, tok_recv, sum_send, sum_recv, hid_send, hid_recv, res_send, res_recv) = rest[2 * parts :]
    steps, rows, width = tokens_ref.shape
    half = width // 2
    count = steps * rows
    tiles = w_in.shape[0]
    units = tiles * 128
    chunks = w_pairs.shape[0]
    per_send = sums_out.shape[3] // 256
    groups = experts // heads
    me = lax.axis_index("expert")
    my_head = lax.axis_index("head")

    weight_copies = [
        pltpu.make_async_copy(gate_up_ref.at[:, 2 * c : 2 * c + 2, :], w_in.at[c], w_sem.at[c]) for c in range(tiles)
    ]
    for copy in weight_copies:
        copy.start()

    barrier = pltpu.get_barrier_semaphore()
    for o in range(1, experts):
        pl.semaphore_signal(barrier, inc=1, device_id={"expert": lax.rem(me + o, experts)}, device_id_type=MESH)
    for o in range(1, heads):
        pl.semaphore_signal(barrier, inc=1, device_id={"head": lax.rem(my_head + o, heads)}, device_id_type=MESH)

    for s in range(steps):
        flat[s * rows : (s + 1) * rows, :] = tokens_ref[s].astype(F32)
    packed[0] = jnp.concatenate([flat[:, :half], flat[:, half:]], axis=0).astype(BF16)

    pl.semaphore_wait(barrier, experts + heads - 2)

    token_copies = []
    for o in range(1, experts):
        copy = pltpu.make_async_remote_copy(
            src_ref=packed.at[0],
            dst_ref=packed.at[o],
            send_sem=tok_send.at[o],
            recv_sem=tok_recv.at[o],
            device_id={"expert": lax.rem(me + o, experts)},
            device_id_type=MESH,
        )
        copy.start()
        token_copies.append(copy)

    eye = lax.broadcasted_iota(jnp.int32, (rows, rows), 0) == lax.broadcasted_iota(jnp.int32, (rows, rows), 1)
    for s in range(steps):
        scores = scores_ref[s]
        weights = 2.5 * scores / jnp.sum(scores, axis=0, keepdims=True)
        for b in range(experts):
            slot = lax.rem(me + b, experts) // span
            row = jnp.sum(jnp.where(routes_ref[s] == slot, weights, 0.0), axis=0, keepdims=True)
            column = jnp.sum(jnp.where(eye, jnp.broadcast_to(row, (rows, rows)), 0.0), axis=1, keepdims=True)
            column = jnp.broadcast_to(column, (rows, 128))
            share[b, s * rows : (s + 1) * rows, :] = column
            share[b, count + s * rows : count + (s + 1) * rows, :] = column

    for c in range(chunks):
        weight_copies[2 * c].wait()
        weight_copies[2 * c + 1].wait()
        w_pairs[c] = jnp.concatenate([w_in[2 * c + i].reshape(2 * width, 128) for i in range(2)], axis=1)
    down_copy = pltpu.make_async_copy(down_ref, w_out, down_sem)
    down_copy.start()

    lane = lax.broadcasted_iota(jnp.int32, (128, 512), 1)
    feature = lax.broadcasted_iota(jnp.int32, (128, 512), 0)
    place = jnp.where(lane < 256, 2 * feature, 2 * feature + 257)
    selector = jnp.where(lane == place, 1.0, 0.0).astype(BF16)
    per_half = half // 128
    for b in range(experts):
        if b:
            token_copies[b - 1].wait_recv()
        block = packed[b]
        stack = jnp.concatenate([block[:, 128 * j : 128 * j + 128] for j in range(per_half)], axis=0)
        wide = jnp.dot(stack, selector, preferred_element_type=F32)
        for j in range(per_half):
            for k in range(2):
                piece = wide[16 * j + 8 * k : 16 * j + 8 * k + 8]
                pair = jnp.concatenate([piece[:, :256], piece[:, 256:]], axis=0).astype(BF16)
                at = 256 * (k * per_half + j)
                spread[16 * b : 16 * b + 16, at : at + 256] = pair

    sum_copies = []
    for c in range(chunks):
        part = jnp.dot(spread[...], w_pairs[c], preferred_element_type=F32)
        part = part.reshape(heads, 16 * groups, 256)
        sums[:, :, 256 * c : 256 * c + 256] = part
        n, k = c // per_send, c % per_send
        sums_out[:, n, :, 256 * k : 256 * k + 256] = part.astype(BF16)
        if k == per_send - 1:
            for o in range(1, heads):
                peer = lax.rem(my_head + o, heads)
                copy = pltpu.make_async_remote_copy(
                    src_ref=sums_out.at[peer, n],
                    dst_ref=sums_in.at[o - 1, n],
                    send_sem=sum_send.at[o - 1, n],
                    recv_sem=sum_recv.at[o - 1, n],
                    device_id={"head": peer},
                    device_id_type=MESH,
                )
                copy.start()
                sum_copies.append(copy)

    for copy in sum_copies:
        copy.wait_recv()
    sends = sums_out.shape[1]
    total = sums[my_head]
    for o in range(1, heads):
        total += jnp.concatenate([sums_in[o - 1, n].astype(F32) for n in range(sends)], axis=1)
    total = total.reshape(groups, 2, 8, units)
    gate, up = total[:, 0], total[:, 1]
    hidden = gate / (1.0 + jnp.exp(-gate)) * up
    hidden = jnp.stack([hidden[:, :, : units // 2], hidden[:, :, units // 2 :]], axis=1)
    hidden_all[my_head] = hidden.reshape(16 * groups, units // 2).astype(BF16)
    hidden_copies = []
    for o in range(1, heads):
        copy = pltpu.make_async_remote_copy(
            src_ref=hidden_all.at[my_head],
            dst_ref=hidden_all.at[my_head],
            send_sem=hid_send.at[o - 1],
            recv_sem=hid_recv.at[o - 1],
            device_id={"head": lax.rem(my_head + o, heads)},
            device_id_type=MESH,
        )
        copy.start()
        hidden_copies.append(copy)
    down_copy.wait()
    for copy in hidden_copies:
        copy.wait_recv()

    blocks = hidden_all[...].astype(F32).reshape(experts, 2, 8, units // 2)
    left = jnp.concatenate([blocks[:, 0], blocks[:, 1]], axis=2).reshape(8 * experts, units).astype(BF16)
    result_copies = []
    at = 0
    for n in range(parts):
        size = results_out[n].shape[2]
        low = jnp.dot(left, w_out[:, at : at + size], preferred_element_type=F32)
        high = jnp.dot(left, w_out[:, half + at : half + at + size], preferred_element_type=F32)
        both = jnp.concatenate([low.reshape(experts, 8, size), high.reshape(experts, 8, size)], axis=1)
        own[:, at : at + size] = both[0]
        results_out[n][...] = both.astype(BF16)
        for b in range(1, experts):
            copy = pltpu.make_async_remote_copy(
                src_ref=results_out[n].at[b],
                dst_ref=results_in[n].at[b],
                send_sem=res_send.at[b, n],
                recv_sem=res_recv.at[b, n],
                device_id={"expert": lax.rem(me - b + experts, experts)},
                device_id_type=MESH,
            )
            copy.start()
            result_copies.append(copy)
        at += size

    at = 0
    for n in range(parts):
        size = results_out[n].shape[2]
        mixed = share[0][:, :1] * own[:, at : at + size]
        for b in range(1, experts):
            result_copies[n * (experts - 1) + b - 1].wait_recv()
            mixed += share[b][:, :1] * results_in[n][b].astype(F32)
        for s in range(steps):
            for k in range(2):
                rows_at = k * count + s * rows
                to = k * half + at
                out_ref[s, :, to : to + size] = mixed[rows_at : rows_at + rows].astype(BF16)
        at += size

    for copy in token_copies + sum_copies + hidden_copies + result_copies:
        copy.wait_send()


def body(experts, heads, tokens, gate_scores, route_copy, gate_up, down_proj):
    steps, rows, width = tokens.shape
    units = gate_up.shape[3]
    span = max(1, experts // 16)
    count = steps * rows
    half = width // 2
    tiles = units // 128
    chunks = units // 256
    groups = experts // heads
    per_send = min(2, chunks)
    sends = chunks // per_send
    assert count == 8 and experts % heads == 0 and units % 256 == 0 and half % 128 == 0
    gate_up = gate_up.reshape(width, 2, tiles, 128).transpose(0, 2, 1, 3).reshape(width, 2 * tiles, 128)
    down = down_proj.reshape(units, width)
    parts = widths_of(half)
    vmem, hbm = pl.BlockSpec(memory_space=pltpu.VMEM), pl.BlockSpec(memory_space=pl.ANY)
    dma = pltpu.SemaphoreType.DMA
    flops = 2 * 8 * experts * width * units * 3
    return pl.pallas_call(
        functools.partial(fused, experts, heads, span),
        out_shape=jax.ShapeDtypeStruct(tokens.shape, tokens.dtype),
        in_specs=[vmem, vmem, vmem, hbm, hbm],
        out_specs=vmem,
        scratch_shapes=[
            pltpu.VMEM((tiles, width, 2, 128), BF16),
            pltpu.VMEM((chunks, 2 * width, 256), BF16),
            pltpu.VMEM((units, width), BF16),
            pltpu.VMEM((8, width), F32),
            pltpu.VMEM((experts, 16, half), BF16),
            pltpu.VMEM((16 * experts, 2 * width), BF16),
            pltpu.VMEM((experts, 16, 128), F32),
            pltpu.VMEM((heads, 16 * groups, units), F32),
            pltpu.VMEM((heads, sends, 16 * groups, 256 * per_send), BF16),
            pltpu.VMEM((heads - 1, sends, 16 * groups, 256 * per_send), BF16),
            pltpu.VMEM((heads, 16 * groups, units // 2), BF16),
            pltpu.VMEM((16, half), F32),
        ]
        + [pltpu.VMEM((experts, 16, size), BF16) for size in parts] * 2
        + [
            dma((tiles,)),
            dma,
            dma((experts,)),
            dma((experts,)),
            dma((heads - 1, sends)),
            dma((heads - 1, sends)),
            dma((heads - 1,)),
            dma((heads - 1,)),
            dma((experts, len(parts))),
            dma((experts, len(parts))),
        ],
        compiler_params=pltpu.CompilerParams(
            collective_id=0, has_side_effects=True, vmem_limit_bytes=56 * 2**20
        ),
        cost_estimate=pl.CostEstimate(
            flops=flops, bytes_accessed=6 * width * units, transcendentals=8 * groups * units
        ),
    )(tokens, gate_scores.transpose(0, 2, 1), route_copy.transpose(0, 2, 1), gate_up, down)


def solution(mesh):
    experts, heads = mesh.shape["expert"], mesh.shape["head"]
    return jax.shard_map(
        functools.partial(body, experts, heads),
        mesh=mesh,
        in_specs=(
            P(None, ("groups", "expert"), "head"),
            P(None, ("groups", "expert"), None),
            P(None, ("groups", "expert"), None),
            P("expert", "head", None, None),
            P("expert", None, "head"),
        ),
        out_specs=P(None, ("groups", "expert"), "head"),
        check_vma=False,
    )
```

time: 110 us -> 25.5 us (0.23)
  waiting for transfers between devices: 41.8 us -> 0 us
  Pallas kernels: 0 us -> 23.8 us
  starting transfers between devices: 19.3 us -> 0 us
  matrix products: 18.4 us -> 0 us
  between operations: 13.5 us -> 0.01 us
  local copies, waits for them, and re-layouts: 12.5 us -> 1.37 us
  other arithmetic: 3.74 us -> 0 us
    psum x1 -> x0, waiting for transfers between devices: 32.8 us -> none  [body(): total = lax.psum(expert_gated, 'head')]
    pallas_call x0 -> x1, Pallas kernels: none -> 23.8 us  [body(): pl.pallas_call(functools.partial(fused, experts, heads, span), out_shape=...]
    all_to_all x4 -> x0, starting transfers between devices: 19.3 us -> none  [the longest x2 11.4 us: body(): lax.all_to_all(outgoing, 'expert', split_axis=0, concat_axis=0, tiled=True)]
    dot_general x8 -> x0, matrix products: 18.4 us -> none  [the longest x2 9.59 us: body(): jnp.dot(rows_in.reshape(-1, quarter), w_in, preferred_element_type=jnp.fl...]
    all_to_all x4 -> x0, waiting for transfers between devices: 9 us -> none  [the longest x2 8.1 us: body(): lax.all_to_all(partial_value, 'expert', split_axis=0, concat_axis=0, tile...]
    unnamed x3 -> x1, local copies, waits for them, and re-layouts: 9.31 us -> 1.37 us
    another operation x2 -> x0, local copies, waits for them, and re-layouts: 1.27 us -> none  [body(): outgoing = outgoing.reshape(device_count, route_item_count, quarter)]
  transfers between devices with their start and end apart: 5 -> 0, of which waited for: 4 -> 0; matrix products, arithmetic and copies ran while one was open for 20% -> 0% of each run, Pallas kernels for 0% -> 0%
where the time goes in v1:
time: 25.5 us; the launch traced here: 25.2 us
  Pallas kernels  23.8 us (93%)
  local copies, waits for them, and re-layouts  1.37 us (5%)
    pallas_call x1, Pallas kernels, body(): pl.pallas_call(functools.partial(fused, experts, heads, span), out_shape=...  23.8 us
    unnamed x1, local copies, waits for them, and re-layouts  1.37 us

profile of v1, /device:TPU:0, one launch (start us, length us, event | category | flops | bytes accessed | tf_op | source)
XLA Modules:
  0.0 25.2 jit_solution(6110579581021902641)
XLA Ops:
  0.0 23.8 %shard_map.55 = bf16[2,4,1792]{2,1,0:T(4,128)(2,1)} custom-call(bf16[2,4,1792]{2,1,0:T(4,128)(2,1)} %tokens_ref.1, f32[2,2,4]{2,1,0:T(2,128)} %bitcast.10, s32[2,2,4]{2,1,0:T(2,128)} %bitcast.11, bf16[1792,16,128]{2,1,0:T(8,128)(2,1)} %bitcast.8, bf16[1024,1792]{1,0:T(8,128)(2,1)} %bitcast.9), custom_call_target="tpu_custom_call" | custom-call | flops 352321536 | bytes 11010048 | tf_op jit(solution)/shard_map/pallas_call | solution.py:233
  23.8 1.4 %copy.8 = bf16[2,4,1792]{2,1,0:T(4,128)(2,1)} copy(bf16[2,4,1792]{2,1,0:T(4,128)(2,1)} %shard_map.55) | data formatting | bytes 57344

commit v2 on v1

--- a/solution.py
+++ b/solution.py
@@ -38,11 +38,14 @@
     sums_in,
     hidden_all,
     own,
+    tokens_in,
+    scores_in,
+    routes_in,
     *rest,
 ):
-    parts = (len(rest) - 10) // 2
+    parts = (len(rest) - 11) // 2
     results_out, results_in = rest[:parts], rest[parts : 2 * parts]
-    (w_sem, down_sem, tok_send, tok_recv, sum_send, sum_recv, hid_send, hid_recv, res_send, res_recv) = rest[2 * parts :]
+    (w_sem, down_sem, tok_send, tok_recv, sum_send, sum_recv, hid_send, hid_recv, res_send, res_recv, in_sem) = rest[2 * parts :]
     steps, rows, width = tokens_ref.shape
     half = width // 2
     count = steps * rows
@@ -54,20 +57,27 @@
     me = lax.axis_index("expert")
     my_head = lax.axis_index("head")
 
+    barrier = pltpu.get_barrier_semaphore()
+    for o in range(1, experts):
+        pl.semaphore_signal(barrier, inc=1, device_id={"expert": lax.rem(me + o, experts)}, device_id_type=MESH)
+    for o in range(1, heads):
+        pl.semaphore_signal(barrier, inc=1, device_id={"head": lax.rem(my_head + o, heads)}, device_id_type=MESH)
+
+    small_copies = [
+        pltpu.make_async_copy(src, dst, in_sem.at[n])
+        for n, (src, dst) in enumerate(((tokens_ref, tokens_in), (scores_ref, scores_in), (routes_ref, routes_in)))
+    ]
+    for copy in small_copies:
+        copy.start()
     weight_copies = [
         pltpu.make_async_copy(gate_up_ref.at[:, 2 * c : 2 * c + 2, :], w_in.at[c], w_sem.at[c]) for c in range(tiles)
     ]
     for copy in weight_copies:
         copy.start()
 
-    barrier = pltpu.get_barrier_semaphore()
-    for o in range(1, experts):
-        pl.semaphore_signal(barrier, inc=1, device_id={"expert": lax.rem(me + o, experts)}, device_id_type=MESH)
-    for o in range(1, heads):
-        pl.semaphore_signal(barrier, inc=1, device_id={"head": lax.rem(my_head + o, heads)}, device_id_type=MESH)
-
+    small_copies[0].wait()
     for s in range(steps):
-        flat[s * rows : (s + 1) * rows, :] = tokens_ref[s].astype(F32)
+        flat[s * rows : (s + 1) * rows, :] = tokens_in[s].astype(F32)
     packed[0] = jnp.concatenate([flat[:, :half], flat[:, half:]], axis=0).astype(BF16)
 
     pl.semaphore_wait(barrier, experts + heads - 2)
@@ -85,13 +95,15 @@
         copy.start()
         token_copies.append(copy)
 
+    small_copies[1].wait()
+    small_copies[2].wait()
     eye = lax.broadcasted_iota(jnp.int32, (rows, rows), 0) == lax.broadcasted_iota(jnp.int32, (rows, rows), 1)
     for s in range(steps):
-        scores = scores_ref[s]
+        scores = scores_in[s]
         weights = 2.5 * scores / jnp.sum(scores, axis=0, keepdims=True)
         for b in range(experts):
             slot = lax.rem(me + b, experts) // span
-            row = jnp.sum(jnp.where(routes_ref[s] == slot, weights, 0.0), axis=0, keepdims=True)
+            row = jnp.sum(jnp.where(routes_in[s] == slot, weights, 0.0), axis=0, keepdims=True)
             column = jnp.sum(jnp.where(eye, jnp.broadcast_to(row, (rows, rows)), 0.0), axis=1, keepdims=True)
             column = jnp.broadcast_to(column, (rows, 128))
             share[b, s * rows : (s + 1) * rows, :] = column
@@ -233,7 +245,7 @@
     return pl.pallas_call(
         functools.partial(fused, experts, heads, span),
         out_shape=jax.ShapeDtypeStruct(tokens.shape, tokens.dtype),
-        in_specs=[vmem, vmem, vmem, hbm, hbm],
+        in_specs=[hbm] * 5,
         out_specs=vmem,
         scratch_shapes=[
             pltpu.VMEM((tiles, width, 2, 128), BF16),
@@ -248,6 +260,9 @@
             pltpu.VMEM((heads - 1, sends, 16 * groups, 256 * per_send), BF16),
             pltpu.VMEM((heads, 16 * groups, units // 2), BF16),
             pltpu.VMEM((16, half), F32),
+            pltpu.VMEM(tokens.shape, BF16),
+            pltpu.VMEM((steps, route_copy.shape[2], rows), F32),
+            pltpu.VMEM((steps, route_copy.shape[2], rows), jnp.int32),
         ]
         + [pltpu.VMEM((experts, 16, size), BF16) for size in parts] * 2
         + [
@@ -261,6 +276,7 @@
             dma((heads - 1,)),
             dma((experts, len(parts))),
             dma((experts, len(parts))),
+            dma((3,)),
         ],
         compiler_params=pltpu.CompilerParams(
             collective_id=0, has_side_effects=True, vmem_limit_bytes=56 * 2**20

time: 25.5 us -> 24.6 us (0.965)
  Pallas kernels: 23.8 us -> 23.1 us
    pallas_call x1, Pallas kernels: 23.8 us -> 23.1 us  [body(): pl.pallas_call(functools.partial(fused, experts, heads, span), out_shape=...]
where the time goes in v2:
time: 24.6 us; the launch traced here: 24.5 us
  Pallas kernels  23.1 us (94%)
  local copies, waits for them, and re-layouts  1.37 us (6%)
    pallas_call x1, Pallas kernels, body(): pl.pallas_call(functools.partial(fused, experts, heads, span), out_shape=...  23.1 us
    unnamed x1, local copies, waits for them, and re-layouts  1.37 us

profile of v2, /device:TPU:0, one launch (start us, length us, event | category | flops | bytes accessed | tf_op | source)
XLA Modules:
  0.0 24.5 jit_solution(6690116202495941131)
XLA Ops:
  0.0 23.1 %shard_map.55 = bf16[2,4,1792]{2,1,0:T(4,128)(2,1)} custom-call(bf16[2,4,1792]{2,1,0:T(4,128)(2,1)} %tokens_ref.1, f32[2,2,4]{2,1,0:T(2,128)} %bitcast.10, s32[2,2,4]{2,1,0:T(2,128)} %bitcast.11, bf16[1792,16,128]{2,1,0:T(8,128)(2,1)} %bitcast.8, bf16[1024,1792]{1,0:T(8,128)(2,1)} %bitcast.9), custom_call_target="tpu_custom_call" | custom-call | flops 352321536 | bytes 11010048 | tf_op jit(solution)/shard_map/pallas_call | solution.py:245
  23.1 1.4 %copy.8 = bf16[2,4,1792]{2,1,0:T(4,128)(2,1)} copy(bf16[2,4,1792]{2,1,0:T(4,128)(2,1)} %shard_map.55) | data formatting | bytes 57344

commit v3 on v2

--- a/solution.py
+++ b/solution.py
@@ -12,8 +12,9 @@
 
 
 def widths_of(half):
-    first = ((half // 128 + 1) // 2) * 128
-    return [w for w in (first, half - first) if w]
+    tiles = half // 128
+    big = tiles // 2
+    return [128 * w for w in (big, big, tiles - 2 * big) if w]
 
 
 def fused(

time: 24.6 us -> 24.7 us (level)
  no operation moved by 1% of the time
where the time goes in v3:
time: 24.7 us; the launch traced here: 24.5 us
  Pallas kernels  23.1 us (94%)
  local copies, waits for them, and re-layouts  1.37 us (6%)
    pallas_call x1, Pallas kernels, body(): pl.pallas_call(functools.partial(fused, experts, heads, span), out_shape=...  23.1 us
    unnamed x1, local copies, waits for them, and re-layouts  1.37 us

profile of v3, /device:TPU:0, one launch (start us, length us, event | category | flops | bytes accessed | tf_op | source)
XLA Modules:
  0.0 24.5 jit_solution(6893549506535111496)
XLA Ops:
  0.0 23.1 %shard_map.55 = bf16[2,4,1792]{2,1,0:T(4,128)(2,1)} custom-call(bf16[2,4,1792]{2,1,0:T(4,128)(2,1)} %tokens_ref.1, f32[2,2,4]{2,1,0:T(2,128)} %bitcast.10, s32[2,2,4]{2,1,0:T(2,128)} %bitcast.11, bf16[1792,16,128]{2,1,0:T(8,128)(2,1)} %bitcast.8, bf16[1024,1792]{1,0:T(8,128)(2,1)} %bitcast.9), custom_call_target="tpu_custom_call" | custom-call | flops 352321536 | bytes 11010048 | tf_op jit(solution)/shard_map/pallas_call | solution.py:246
  23.1 1.4 %copy.8 = bf16[2,4,1792]{2,1,0:T(4,128)(2,1)} copy(bf16[2,4,1792]{2,1,0:T(4,128)(2,1)} %shard_map.55) | data formatting | bytes 57344
